TPU v7x, 128 devices: a whole 4x4x4 slice. The times are simulated.
128 devices in a mesh: dp: 4 (over y), item: 32 (over z, x, core).
Axes of the slice: x: 4, y: 4, z: 4, core: 2. Of those that a mesh axis runs over, the one named last changes fastest.
Arguments:
- queries: bfloat16 [131072, 256], P(('dp', 'item')), may hold values from -0.5 to 0.5
- item_table: float32 [131072, 256], P('item'), may hold values from -0.5 to 0.5
- adagrad_state: float32 [131072], P('item'), may hold values from 1 to 1000
- pos_owner: int32 [131072, 1], P(('dp', 'item')), may hold values from 0 to 31; in each aligned block of 1024 rows (0 to 1023, 1024 to 2047, ...) at most 96 rows name the same one
- pos_row: int32 [131072], P(('dp', 'item')), may hold values from 0 to 4095
- neg_rows: int32 [6144], P(('dp', 'item')), may hold values from 0 to 4095
Outputs:
- query_grad: bfloat16 [131072, 256], P(('dp', 'item'))
- example_loss: float32 [131072], P(('dp', 'item'))
- new_table: float32 [131072, 256], P('item')
- new_state: float32 [131072], P('item')
Inputs may be any that keep to these rules, and one draw needn't show every extreme that they name: `pos_owner`: within the rows of one device (aligned blocks of 1024 examples) no shard is named more than 96 times; some device's block names one shard exactly 96 times.
All inputs are finite; a program needn't handle non-finite values.
Results may differ from a plain program's by a relative error of at most 0.0049.
Values may be sent and summed in bfloat16 or wider, within the bound.
A program may use at most 64 MiB of HBM per device.

v0:
```python
import math
import jax
import jax.numpy as jnp
from jax import lax
from jax.sharding import PartitionSpec as P

INV_TEMP = 20.0
LEARN_RATE = 0.05
EPSILON = 1e-06


def unit_rows(matrix):
    row_norm = jnp.sqrt(jnp.sum(matrix * matrix, axis=-1, keepdims=True) + EPSILON)
    return (matrix / row_norm, row_norm)


def on_device(queries, item_table, adagrad_state, pos_owner, pos_row, neg_rows):
    ex_count = queries.shape[0]
    rows_dev = item_table.shape[0]
    feat_width = item_table.shape[1]
    item_count = lax.axis_size("item")
    capacity = 3 * ex_count // item_count
    item_index = lax.axis_index("item")
    query_hat, query_norm = unit_rows(queries.astype(jnp.float32))
    query_send = query_hat.astype(jnp.bfloat16)
    unit_table, table_norm = unit_rows(item_table)
    table_send = unit_table.astype(jnp.bfloat16)
    owners = pos_owner[:, 0]
    onehot = (owners[:, None] == jnp.arange(item_count, dtype=jnp.int32)[None, :]).astype(jnp.int32)
    earlier = jnp.cumsum(onehot, axis=0) - onehot
    slots = jnp.sum(earlier * onehot, axis=1)
    places = owners * capacity + slots
    requests = jnp.zeros((item_count * capacity,), jnp.int32).at[places].set(pos_row)
    requests = requests.reshape(item_count, capacity)
    asked_rows = lax.all_to_all(requests, "item", split_axis=0, concat_axis=0, tiled=True)
    found = table_send[asked_rows]
    returned = lax.all_to_all(found, "item", split_axis=0, concat_axis=0, tiled=True)
    pos_e = returned.reshape(item_count * capacity, feat_width)[places]
    pos_gid = owners * rows_dev + pos_row
    my_gid = item_index * rows_dev + neg_rows
    my_neg = table_send[neg_rows]
    block_rows, block_ids = (
        lax.all_gather(my_neg, "item", axis=0, tiled=True),
        lax.all_gather(my_gid, "item", axis=0, tiled=True),
    )
    all_rows, all_ids = (
        lax.all_gather(block_rows, "dp", axis=0, tiled=True),
        lax.all_gather(block_ids, "dp", axis=0, tiled=True),
    )
    negs = all_rows.shape[0]
    block_size = math.gcd(negs, 1024)
    block_count = negs // block_size
    row_blocks = all_rows.reshape(block_count, block_size, feat_width)
    id_blocks = all_ids.reshape(block_count, block_size)

    def block_scores(row_block, id_block):
        scores = (
            jnp.einsum("ed,nd->en", query_send, row_block, preferred_element_type=jnp.float32)
            * INV_TEMP
        )
        allowed = id_block[None, :] != pos_gid[:, None]
        return (scores, allowed)

    s_pos = INV_TEMP * jnp.sum(query_send.astype(jnp.float32) * pos_e.astype(jnp.float32), axis=1)

    def add_exp(carry, pieces):
        scores, allowed = block_scores(pieces[0], pieces[1])
        return (carry + jnp.sum(jnp.where(allowed, jnp.exp(scores), 0.0), axis=1), None)

    neg_totals, _ = lax.scan(add_exp, jnp.zeros((ex_count,), jnp.float32), (row_blocks, id_blocks))
    lse = jnp.log(jnp.exp(s_pos) + neg_totals)
    example_loss = lse - s_pos

    def both_products(carry, pieces):
        scores, allowed = block_scores(pieces[0], pieces[1])
        probs = jnp.where(allowed, jnp.exp(scores - lse[:, None]), 0.0).astype(jnp.bfloat16)
        carry = carry + jnp.dot(probs, pieces[0], preferred_element_type=jnp.float32)
        partial_rows = INV_TEMP * jnp.einsum(
            "en,ed->nd", probs, query_send, preferred_element_type=jnp.float32
        )
        return (carry, partial_rows)

    neg_part, partial_blocks = lax.scan(
        both_products, jnp.zeros((ex_count, feat_width), jnp.float32), (row_blocks, id_blocks)
    )
    neg_partials = partial_blocks.reshape(negs, feat_width)
    p_pos = jnp.exp(s_pos - lse)
    g_query = INV_TEMP * ((p_pos - 1.0)[:, None] * pos_e.astype(jnp.float32) + neg_part)
    query_grad = (
        (g_query - query_hat * jnp.sum(query_hat * g_query, axis=1, keepdims=True)) / query_norm
    ).astype(jnp.bfloat16)
    g_pos = INV_TEMP * (p_pos - 1.0)[:, None] * query_hat
    outbox = jnp.zeros((item_count * capacity, feat_width), jnp.float32).at[places].set(g_pos)
    outbox = outbox.reshape(item_count, capacity, feat_width)
    inbox = lax.all_to_all(
        outbox.astype(jnp.bfloat16), "item", split_axis=0, concat_axis=0, tiled=True
    ).astype(outbox.dtype)
    dense = jnp.zeros((rows_dev, feat_width), jnp.float32)
    dense = dense.at[asked_rows.reshape(-1)].add(inbox.reshape(-1, feat_width))
    neg_grad = lax.psum_scatter(neg_partials, ("dp", "item"), scatter_dimension=0, tiled=True)
    dense = dense.at[neg_rows].add(neg_grad)
    g_unit = lax.psum(dense.astype(jnp.bfloat16), "dp").astype(jnp.float32)
    g_row = (g_unit - unit_table * jnp.sum(unit_table * g_unit, axis=1, keepdims=True)) / table_norm
    new_state = adagrad_state + jnp.mean(g_row * g_row, axis=1)
    new_table = item_table - LEARN_RATE * g_row / jnp.sqrt(new_state)[:, None]
    return (query_grad, example_loss, new_table, new_state)


def solution(mesh):
    placed = (
        P(("dp", "item"), None),
        P("item", None),
        P("item"),
        P(("dp", "item"), None),
        P(("dp", "item")),
        P(("dp", "item")),
    )
    return jax.shard_map(
        on_device,
        mesh=mesh,
        in_specs=placed,
        out_specs=(P(("dp", "item"), None), P(("dp", "item")), P("item", None), P("item")),
        check_vma=False,
    )
```

profile of v0, /device:TPU:1, one launch (start us, length us, event | category | flops | bytes accessed | tf_op | source)
XLA Modules:
  0.0 490.1 jit_solution(17192636211847905702)
XLA Ops:
  7.2 3.0 multiply_reduce_fusion.1
  10.7 0.7 fusion.33
  11.4 0.6 dynamic-slice
  12.8 0.7 gather_fusion.2
  13.5 29.8 %all-gather = bf16[1536,256]{1,0:T(8,128)(2,1)} all-gather(bf16[48,256]{1,0:T(8,128)(2,1)S(1)} %gather_fusion.2), channel_id=2, replica_groups=mesh['dp'=4,'item'=32] {'item'}, dimensions={0}, use_global_device_ids=true | all-gather | bytes 811008 | tf_op jit(solution)/shard_map/all_gather | solution.py:43
  43.3 9.0 %reduce-window.6 = s32[32,8,128]{2,1,0:T(8,128)S(1)} reduce-window(s32[32,8,128]{2,1,0:T(8,128)S(1)} %fusion.29, s32[]{:T(128)} %constant.33.clone.1), window={size=1x1x128 pad=0_0x0_0x127_0}, to_apply=%region_2.0 | reduce-window | flops 4161536 | bytes 262148 | tf_op jit(solution)/shard_map/reduce-window
  52.8 4.3 scatter_custom_fusion
  57.2 11.8 %all_to_all.22 = s32[32,1,96]{2,1,0:T(1,128)S(1)} all-to-all(s32[32,1,96]{2,1,0:T(1,128)S(1)} %all_to_all.14), channel_id=1, replica_groups=mesh['dp'=4,'item'=32] {'item'}, dimensions={0} | all-to-all | bytes 24576 | tf_op jit(solution)/shard_map/all_to_all | solution.py:35
  69.1 13.0 %gather_fusion = bf16[3072,256]{1,0:T(8,128)(2,1)} fusion(bf16[4096,256]{1,0:T(8,128)(2,1)S(1)} %fusion.33, s32[3072]{0:T(1024)S(1)} %broadcast_clamp_fusion), kind=kCustom, calls=%fused_computation | custom fusion | bytes 3158016 | tf_op jit(solution)/shard_map/gather | solution.py:36
  82.2 4.3 all-to-all-start.1
  86.6 28.8 %all-reduce = s32[1536]{0:T(1024)S(1)} all-reduce(s32[1536]{0:T(1024)S(1)} %get-tuple-element.167), channel_id=1, replica_groups=mesh['dp'=4,'item'=32] {'item'}, use_global_device_ids=true, to_apply=%add | all-reduce | flops 1536 | bytes 12288
  115.4 9.7 %all-gather.2 = s32[4,1,1536]{2,1,0:T(1,128)S(1)} all-gather(s32[1,1,1536]{2,1,0:T(1,128)S(1)} %reshape.204), channel_id=1, replica_groups=mesh['dp'=4,'item'=32] {'dp'}, dimensions={0}, use_global_device_ids=true | all-gather | bytes 30720 | tf_op jit(solution)/shard_map/all_gather | solution.py:48
  125.5 3.9 gather_fusion.1
  129.9 12.9 %while.24 = (s32[]{:T(128)}, f32[1024]{0:T(1024)S(1)}, s32[6,1024]{1,0:T(8,128)S(1)}, s32[1024]{0:T(1024)S(1)}, bf16[6,1024,256]{2,1,0:T(8,128)(2,1)}, /*index=5*/bf16[1024,256]{1,0:T(8,128)(2,1)S(1)}, s32[]{:T(128)}, s32[]{:T(128)}) while((s32[]{:T(128)}, f32[1024]{0:T(1024)S(1)}, s32[6,1024]{1,0:T(8,128)S(1)}, ...), condition=%wide.region_9.10_spmd.clone, body=%wide.region_7.9_spmd.clone.sunk | while | flops 541066240 | bytes 1081955 | solution.py:70
  130.0 2.2 fusion.54
  132.2 2.1 fusion.54
  134.3 2.1 fusion.54
  136.4 2.1 fusion.54
  138.6 2.1 fusion.54
  140.7 2.1 fusion.54
  142.8 0.6 broadcast_multiply_fusion
  143.4 48.0 %while.25 = (s32[]{:T(128)}, f32[1024,256]{1,0:T(8,128)S(1)}, f32[6,1024,256]{2,1,0:T(8,128)}, s32[6,1024]{1,0:T(8,128)S(1)}, s32[1024]{0:T(1024)S(1)}, /*index=...) while((s32[]{:T(128)}, f32[1024,256]{1,0:T(8,128)S(1)}, ...), condition=%wide.region_11.12_spmd.clone, body=%wide.region_10.11_spmd.clone.sunk | while | flops 1616642048 | bytes 19945104 | solution.py:83
  143.4 2.1 fusion.61
  145.6 1.3 copy-done.12
  146.9 1.7 fusion.62
  148.6 2.8 convolution_add_fusion.2
  151.4 2.1 fusion.61
  153.6 1.3 copy-done.12
  154.9 1.8 fusion.62
  156.7 2.8 convolution_add_fusion.2
  159.5 2.1 fusion.61
  161.7 1.3 copy-done.12
  163.0 1.7 fusion.62
  164.7 2.8 convolution_add_fusion.2
  167.5 2.1 fusion.61
  169.6 1.3 copy-done.12
  171.0 1.7 fusion.62
  172.7 2.8 convolution_add_fusion.2
  175.5 2.1 fusion.61
  177.6 1.3 copy-done.12
  178.9 1.7 fusion.62
  180.6 2.8 convolution_add_fusion.2
  183.5 2.1 fusion.61
  185.6 1.3 copy-done.12
  186.9 1.7 fusion.62
  188.7 2.8 convolution_add_fusion.2
  191.5 7.1 %scatter_custom_fusion.1 = f32[3072,256]{1,0:T(8,128)} fusion(s32[1024]{0:T(1024)S(1)} %bitcast.102, f32[]{:T(128)} %constant.31.clone.1, f32[1024]{0:T(1024)S(1)} %get-tuple-element.160, bf16[1024,256]{1,0:T(8,128)(2,1)S(1)} %copy-done.3, f32[1024]{0:T(1024)S(1)} %add_sqrt_fusion.1), kind=kCustom, calls=%fused_computation.38 | custom fusion | flops 786432 | bytes 3678212 | tf_op jit(solution)/shard_map/scatter | solution.py:93
  198.6 3.2 convert_element_type.50
  201.8 10.0 %all-to-all-start.2 = ((bf16[32,96,256]{2,1,0:T(8,128)(2,1)}), bf16[32,96,256]{2,1,0:T(8,128)(2,1)S(1)}, u32[]{:S(2)}, u32[]{:S(2)}) async-start(bf16[32,96,256]{2,1,0:T(8,128)(2,1)} %bitcast.89), calls=%async_computation.2 | async-start | bytes 3145728 | tf_op jit(solution)/shard_map/all_to_all | solution.py:95
  211.9 0.5 broadcast.160
  212.4 0.7 reduce.4
  213.2 20.9 %all-to-all-done.2 = bf16[32,96,256]{2,1,0:T(8,128)(2,1)S(1)} async-done(((bf16[32,96,256]{2,1,0:T(8,128)(2,1)}), bf16[32,96,256]{2,1,0:T(8,128)(2,1)S(1)}, u32[]{:S(2)}, u32[]{:S(2)}) %all-to-all-start.2) | async-done | bytes 1572896 | tf_op jit(solution)/shard_map/all_to_all | solution.py:95
  234.1 22.4 %scatter_custom_fusion.2 = f32[4096,256]{1,0:T(8,128)} fusion(s32[3072]{0:T(1024)S(1)} %bitcast.103, bf16[3072,256]{1,0:T(8,128)(2,1)S(1)} %bitcast.88, f32[]{:T(128)} %constant.31.clone.1), kind=kCustom, calls=%fused_computation.34 | custom fusion | flops 1572864 | bytes 5767172 | tf_op jit(solution)/shard_map/scatter-add | solution.py:99
  256.5 148.0 %reduce-scatter.2.cloned.1.call-done = f32[48,256]{1,0:T(8,128)} async-done(((f32[6144,256]{1,0:T(8,128)}), f32[48,256]{1,0:T(8,128)}) %reduce-scatter.2.cloned.1.call-update) | async-done | bytes 49168 | tf_op jit(solution)/shard_map/reduce_scatter | solution.py:100
  404.5 5.2 %scatter_fusion = f32[4096,256]{1,0:T(8,128)} fusion(f32[4096,256]{1,0:T(8,128)} %scatter_custom_fusion.2, s32[48]{0:T(128)S(1)} %get-tuple-element.166, f32[48,256]{1,0:T(8,128)} %reduce-scatter.2.cloned.1.call-done), kind=kCustom, calls=%fused_computation.6 | custom fusion | flops 12288 | bytes 147648 | tf_op jit(solution)/shard_map/scatter-add | solution.py:101
  409.8 3.8 convert_element_type.52
  413.6 0.5 multiply_reduce_fusion.2
  414.1 1.3 divide_convert_fusion
  415.3 56.3 %all-reduce.3.cloned.1.call-done = bf16[4096,256]{1,0:T(8,128)(2,1)} async-done(((bf16[4096,256]{1,0:T(8,128)(2,1)}), bf16[4096,256]{1,0:T(8,128)(2,1)}) %all-reduce.3.cloned.1.call-update) | async-done | bytes 2097168 | tf_op jit(solution)/shard_map/psum | solution.py:102
  471.7 3.9 fusion.13
  475.7 0.7 copy-done.2
  476.4 2.0 multiply_reduce_fusion
  478.4 0.6 fusion.34
  479.0 4.5 divide_subtract_fusion
  (85 shorter events, 2.6 us)
Async XLA Ops:
  7.2 122.8 %all-gather.5.cloned.1.call-start = ((), (), s32[]{:S(2)}) async-start(), calls=%async_computation.6 | async-start | bytes 3932160 | tf_op jit(solution)/shard_map/all_gather | solution.py:47
  7.2 3.5 copy-start
  10.2 1.2 copy-start.11
  10.2 2.5 copy-start.10
  10.2 33.0 %copy-start.7 = (s32[1024,1]{0,1:T(1,128)S(1)}, s32[1024,1]{0,1:T(1,128)}, u32[]{:S(2)}) copy-start(s32[1024,1]{0,1:T(1,128)} %param.13) | copy-start | bytes 12292
  10.7 42.1 %copy-start.9 = (s32[1024]{0:T(1024)S(1)}, s32[1024]{0:T(1024)}, u32[]{:S(2)}) copy-start(s32[1024]{0:T(1024)} %param.14) | copy-start | bytes 12292
  69.1 56.1 %copy-start.3 = (bf16[1024,256]{1,0:T(8,128)(2,1)S(1)}, bf16[1024,256]{1,0:T(8,128)(2,1)}, u32[]{:S(2)}) copy-start(bf16[1024,256]{1,0:T(8,128)(2,1)} %param.10) | copy-start | bytes 1572868
  82.2 43.3 %all-to-all-start.1 = ((bf16[32,96,256]{2,1,0:T(8,128)(2,1)}), bf16[32,96,256]{2,1,0:T(8,128)(2,1)S(1)}, u32[]{:S(2)}, u32[]{:S(2)}) async-start(bf16[32,96,256]{2,1,0:T(8,128)(2,1)} %bitcast.90), calls=%async_computation.1 | async-start | bytes 3145728 | tf_op jit(solution)/shard_map/all_to_all | solution.py:37
  86.5 318.0 %reduce-scatter.2.cloned.1.call-start = ((), (), s32[]{:S(2)}) async-start(), calls=%async_computation.4 | async-start | bytes 6340608 | tf_op jit(solution)/shard_map/reduce_scatter | solution.py:100
  129.9 13.5 %copy-start.4 = (f32[1024,256]{1,0:T(8,128)S(1)}, f32[1024,256]{1,0:T(8,128)}, u32[]{:S(2)}) copy-start(f32[1024,256]{1,0:T(8,128)} %custom-call.1) | copy-start | bytes 3145732
  145.6 1.3 copy-start.12
  153.6 1.3 copy-start.12
  161.6 1.3 copy-start.12
  169.6 1.3 copy-start.12
  177.6 1.3 copy-start.12
  185.6 1.3 copy-start.12
  191.5 7.2 %copy-start.5 = (f32[1024,256]{1,0:T(8,128)}, f32[1024,256]{1,0:T(8,128)S(1)}, u32[]{:S(2)}) copy-start(f32[1024,256]{1,0:T(8,128)S(1)} %get-tuple-element.80) | copy-start | bytes 3145732
  201.8 32.3 %all-to-all-start.2 = ((bf16[32,96,256]{2,1,0:T(8,128)(2,1)}), bf16[32,96,256]{2,1,0:T(8,128)(2,1)S(1)}, u32[]{:S(2)}, u32[]{:S(2)}) async-start(bf16[32,96,256]{2,1,0:T(8,128)(2,1)} %bitcast.89), calls=%async_computation.2 | async-start | bytes 3145728 | tf_op jit(solution)/shard_map/all_to_all | solution.py:95
  211.8 259.9 %all-reduce.3.cloned.1.call-start = ((), (), s32[]{:S(2)}) async-start(), calls=%async_computation.5 | async-start | bytes 4194304 | tf_op jit(solution)/shard_map/psum | solution.py:102
  409.8 3.8 copy-start.6
  471.7 4.1 copy-start.1
  471.7 4.7 copy-start.2
  476.4 2.0 copy-start.8
Sparse Core Ops, SparseCore 0:
  43.4 38.4 all-gather.4
  191.6 212.8 reduce-scatter.1
  413.7 57.9 all-reduce.2
where the time goes:
time: 491 us; the launch traced here: 490 us
  waiting for transfers between devices  225 us (46%)
  blocking collectives  80.1 us (16%)
  other arithmetic  69.7 us (14%)
  matrix products  52.4 us (11%)
  local copies, waits for them, and re-layouts  32.9 us (7%)
  between operations  14.8 us (3%)
  starting transfers between devices  14.4 us (3%)
    reduce_scatter x1, waiting for transfers between devices, on_device(): lax.psum_scatter(neg_partials, ('dp', 'item'), scatter_dimension=0, tiled...  148 us
    psum x1, waiting for transfers between devices, on_device(): g_unit = lax.psum(dense.astype(jnp.bfloat16), 'dp').astype(jnp.float32)  56.3 us
    all_gather x1, blocking collectives, on_device(): lax.all_gather(my_neg, 'item', axis=0, tiled=True)  29.8 us
    unnamed x1, blocking collectives  28.8 us
    dot_general x12, matrix products, block_scores(): jnp.einsum('ed,nd->en', query_send, row_block, preferred_element_type=jnp...  25.4 us
    scatter-add x1, other arithmetic, on_device(): dense = dense.at[asked_rows.reshape(-1)].add(inbox.reshape(-1, feat_width))  22.4 us
    all_to_all x1, waiting for transfers between devices, on_device(): lax.all_to_all(outbox.astype(jnp.bfloat16), 'item', split_axis=0, concat_...  20.9 us
    dot_general x6, matrix products, both_products(): jnp.dot(probs, pieces[0], preferred_element_type=jnp.float32)  16.7 us
  transfers between devices with their start and end apart: 5, of which 3 were waited for; matrix products, arithmetic and copies ran while one was open for 14% of the time, Pallas kernels for 0%

commit v1 on v0

--- a/solution.py
+++ b/solution.py
@@ -99,7 +99,7 @@
     dense = dense.at[asked_rows.reshape(-1)].add(inbox.reshape(-1, feat_width))
     neg_grad = lax.psum_scatter(neg_partials, ("dp", "item"), scatter_dimension=0, tiled=True)
     dense = dense.at[neg_rows].add(neg_grad)
-    g_unit = lax.psum(dense.astype(jnp.bfloat16), "dp").astype(jnp.float32)
+    g_unit = jnp.sum(lax.all_gather(dense.astype(jnp.bfloat16), "dp"), axis=0).astype(jnp.float32)
     g_row = (g_unit - unit_table * jnp.sum(unit_table * g_unit, axis=1, keepdims=True)) / table_norm
     new_state = adagrad_state + jnp.mean(g_row * g_row, axis=1)
     new_table = item_table - LEARN_RATE * g_row / jnp.sqrt(new_state)[:, None]

time: 491 us -> 521 us (1.061)
  waiting for transfers between devices: 225 us -> 250 us
  other arithmetic: 69.7 us -> 75.1 us
    all_gather x0 -> x1, waiting for transfers between devices: none -> 80.7 us  [on_device(): lax.all_gather(dense.astype(jnp.bfloat16), 'dp')]
    psum x1 -> x0, waiting for transfers between devices: 56.3 us -> none  [on_device(): g_unit = lax.psum(dense.astype(jnp.bfloat16), 'dp').astype(jnp.float32)]
    reduce_sum x0 -> x1, other arithmetic: none -> 6.04 us  [on_device(): jnp.sum(lax.all_gather(dense.astype(jnp.bfloat16), 'dp'), axis=0)]
  transfers between devices with their start and end apart: 5 -> 5, of which waited for: 3 -> 3; matrix products, arithmetic and copies ran while one was open for 14% -> 13% of each run, Pallas kernels for 0% -> 0%
where the time goes in v1:
time: 521 us; the launch traced here: 519 us
  waiting for transfers between devices  250 us (48%)
  blocking collectives  80.1 us (15%)
  other arithmetic  75.1 us (14%)
  matrix products  52.4 us (10%)
  local copies, waits for them, and re-layouts  32.4 us (6%)
  between operations  14.8 us (3%)
  starting transfers between devices  14.4 us (3%)
    reduce_scatter x1, waiting for transfers between devices, on_device(): lax.psum_scatter(neg_partials, ('dp', 'item'), scatter_dimension=0, tiled...  148 us
    all_gather x1, waiting for transfers between devices, on_device(): lax.all_gather(dense.astype(jnp.bfloat16), 'dp')  80.7 us
    all_gather x1, blocking collectives, on_device(): lax.all_gather(my_neg, 'item', axis=0, tiled=True)  29.8 us
    unnamed x1, blocking collectives  28.8 us
    dot_general x12, matrix products, block_scores(): jnp.einsum('ed,nd->en', query_send, row_block, preferred_element_type=jnp...  25.4 us
    scatter-add x1, other arithmetic, on_device(): dense = dense.at[asked_rows.reshape(-1)].add(inbox.reshape(-1, feat_width))  22.4 us
    all_to_all x1, waiting for transfers between devices, on_device(): lax.all_to_all(outbox.astype(jnp.bfloat16), 'item', split_axis=0, concat_...  20.9 us
    dot_general x6, matrix products, both_products(): jnp.dot(probs, pieces[0], preferred_element_type=jnp.float32)  16.7 us
  transfers between devices with their start and end apart: 5, of which 3 were waited for; matrix products, arithmetic and copies ran while one was open for 13% of the time, Pallas kernels for 0%

profile of v1, /device:TPU:1, one launch (start us, length us, event | category | flops | bytes accessed | tf_op | source)
XLA Modules:
  0.0 519.4 jit_solution(15889200706058071809)
XLA Ops:
  7.2 3.0 multiply_reduce_fusion.1
  10.7 0.7 fusion.33
  11.4 0.6 dynamic-slice
  12.8 0.7 gather_fusion.2
  13.5 29.8 %all-gather = bf16[1536,256]{1,0:T(8,128)(2,1)} all-gather(bf16[48,256]{1,0:T(8,128)(2,1)S(1)} %gather_fusion.2), channel_id=2, replica_groups=mesh['dp'=4,'item'=32] {'item'}, dimensions={0}, use_global_device_ids=true | all-gather | bytes 811008 | tf_op jit(solution)/shard_map/all_gather | solution.py:43
  43.3 9.0 %reduce-window.6 = s32[32,8,128]{2,1,0:T(8,128)S(1)} reduce-window(s32[32,8,128]{2,1,0:T(8,128)S(1)} %fusion.29, s32[]{:T(128)} %constant.16.clone.1), window={size=1x1x128 pad=0_0x0_0x127_0}, to_apply=%region_2.0 | reduce-window | flops 4161536 | bytes 262148 | tf_op jit(solution)/shard_map/reduce-window
  52.8 4.3 scatter_custom_fusion
  57.2 11.8 %all_to_all.22 = s32[32,1,96]{2,1,0:T(1,128)S(1)} all-to-all(s32[32,1,96]{2,1,0:T(1,128)S(1)} %all_to_all.14), channel_id=1, replica_groups=mesh['dp'=4,'item'=32] {'item'}, dimensions={0} | all-to-all | bytes 24576 | tf_op jit(solution)/shard_map/all_to_all | solution.py:35
  69.1 13.0 %gather_fusion = bf16[3072,256]{1,0:T(8,128)(2,1)} fusion(bf16[4096,256]{1,0:T(8,128)(2,1)S(1)} %fusion.33, s32[3072]{0:T(1024)S(1)} %broadcast_clamp_fusion), kind=kCustom, calls=%fused_computation | custom fusion | bytes 3158016 | tf_op jit(solution)/shard_map/gather | solution.py:36
  82.2 4.3 all-to-all-start.1
  86.6 28.8 %all-reduce = s32[1536]{0:T(1024)S(1)} all-reduce(s32[1536]{0:T(1024)S(1)} %get-tuple-element.167), channel_id=1, replica_groups=mesh['dp'=4,'item'=32] {'item'}, use_global_device_ids=true, to_apply=%add | all-reduce | flops 1536 | bytes 12288
  115.4 9.7 %all-gather.3 = s32[4,1,1536]{2,1,0:T(1,128)S(1)} all-gather(s32[1,1,1536]{2,1,0:T(1,128)S(1)} %reshape.205), channel_id=1, replica_groups=mesh['dp'=4,'item'=32] {'dp'}, dimensions={0}, use_global_device_ids=true | all-gather | bytes 30720 | tf_op jit(solution)/shard_map/all_gather | solution.py:48
  125.5 3.9 gather_fusion.1
  129.9 12.9 %while.24 = (s32[]{:T(128)}, f32[1024]{0:T(1024)S(1)}, s32[6,1024]{1,0:T(8,128)S(1)}, s32[1024]{0:T(1024)S(1)}, bf16[6,1024,256]{2,1,0:T(8,128)(2,1)}, /*index=5*/bf16[1024,256]{1,0:T(8,128)(2,1)S(1)}, s32[]{:T(128)}, s32[]{:T(128)}) while((s32[]{:T(128)}, f32[1024]{0:T(1024)S(1)}, s32[6,1024]{1,0:T(8,128)S(1)}, ...), condition=%wide.region_9.10_spmd.clone, body=%wide.region_7.9_spmd.clone.sunk | while | flops 541066240 | bytes 1081955 | solution.py:70
  130.0 2.2 fusion.54
  132.2 2.1 fusion.54
  134.3 2.1 fusion.54
  136.4 2.1 fusion.54
  138.6 2.1 fusion.54
  140.7 2.1 fusion.54
  142.8 0.6 broadcast_multiply_fusion
  143.4 48.0 %while.25 = (s32[]{:T(128)}, f32[1024,256]{1,0:T(8,128)S(1)}, f32[6,1024,256]{2,1,0:T(8,128)}, s32[6,1024]{1,0:T(8,128)S(1)}, s32[1024]{0:T(1024)S(1)}, /*index=...) while((s32[]{:T(128)}, f32[1024,256]{1,0:T(8,128)S(1)}, ...), condition=%wide.region_11.12_spmd.clone, body=%wide.region_10.11_spmd.clone.sunk | while | flops 1616642048 | bytes 19945104 | solution.py:83
  143.4 2.1 fusion.61
  145.6 1.3 copy-done.11
  146.9 1.7 fusion.62
  148.6 2.8 convolution_add_fusion.2
  151.4 2.1 fusion.61
  153.6 1.3 copy-done.11
  154.9 1.8 fusion.62
  156.7 2.8 convolution_add_fusion.2
  159.5 2.1 fusion.61
  161.7 1.3 copy-done.11
  163.0 1.7 fusion.62
  164.7 2.8 convolution_add_fusion.2
  167.5 2.1 fusion.61
  169.6 1.3 copy-done.11
  171.0 1.7 fusion.62
  172.7 2.8 convolution_add_fusion.2
  175.5 2.1 fusion.61
  177.6 1.3 copy-done.11
  178.9 1.7 fusion.62
  180.6 2.8 convolution_add_fusion.2
  183.5 2.1 fusion.61
  185.6 1.3 copy-done.11
  186.9 1.7 fusion.62
  188.7 2.8 convolution_add_fusion.2
  191.5 7.1 %scatter_custom_fusion.1 = f32[3072,256]{1,0:T(8,128)} fusion(s32[1024]{0:T(1024)S(1)} %bitcast.104, f32[]{:T(128)} %constant.32.clone.1, f32[1024]{0:T(1024)S(1)} %get-tuple-element.160, bf16[1024,256]{1,0:T(8,128)(2,1)S(1)} %copy-done.2, f32[1024]{0:T(1024)S(1)} %add_sqrt_fusion.1), kind=kCustom, calls=%fused_computation.38 | custom fusion | flops 786432 | bytes 3678212 | tf_op jit(solution)/shard_map/scatter | solution.py:93
  198.6 3.2 convert_element_type.52
  201.8 10.0 %all-to-all-start.2 = ((bf16[32,96,256]{2,1,0:T(8,128)(2,1)}), bf16[32,96,256]{2,1,0:T(8,128)(2,1)S(1)}, u32[]{:S(2)}, u32[]{:S(2)}) async-start(bf16[32,96,256]{2,1,0:T(8,128)(2,1)} %bitcast.91), calls=%async_computation.2 | async-start | bytes 3145728 | tf_op jit(solution)/shard_map/all_to_all | solution.py:95
  211.9 0.5 broadcast.160
  212.4 0.7 reduce.5
  213.2 20.9 %all-to-all-done.2 = bf16[32,96,256]{2,1,0:T(8,128)(2,1)S(1)} async-done(((bf16[32,96,256]{2,1,0:T(8,128)(2,1)}), bf16[32,96,256]{2,1,0:T(8,128)(2,1)S(1)}, u32[]{:S(2)}, u32[]{:S(2)}) %all-to-all-start.2) | async-done | bytes 1572896 | tf_op jit(solution)/shard_map/all_to_all | solution.py:95
  234.1 22.4 %scatter_custom_fusion.2 = f32[4096,256]{1,0:T(8,128)} fusion(s32[3072]{0:T(1024)S(1)} %bitcast.105, bf16[3072,256]{1,0:T(8,128)(2,1)S(1)} %bitcast.90, f32[]{:T(128)} %constant.32.clone.1), kind=kCustom, calls=%fused_computation.34 | custom fusion | flops 1572864 | bytes 5767172 | tf_op jit(solution)/shard_map/scatter-add | solution.py:99
  256.5 148.0 %reduce-scatter.2.cloned.1.call-done = f32[48,256]{1,0:T(8,128)} async-done(((f32[6144,256]{1,0:T(8,128)}), f32[48,256]{1,0:T(8,128)}) %reduce-scatter.2.cloned.1.call-update) | async-done | bytes 49168 | tf_op jit(solution)/shard_map/reduce_scatter | solution.py:100
  404.5 5.2 %scatter_fusion = f32[4096,256]{1,0:T(8,128)} fusion(f32[4096,256]{1,0:T(8,128)} %scatter_custom_fusion.2, s32[48]{0:T(128)S(1)} %get-tuple-element.166, f32[48,256]{1,0:T(8,128)} %reduce-scatter.2.cloned.1.call-done), kind=kCustom, calls=%fused_computation.6 | custom fusion | flops 12288 | bytes 147648 | tf_op jit(solution)/shard_map/scatter-add | solution.py:101
  409.8 3.9 convert_element_type.54
  413.7 0.5 multiply_reduce_fusion.2
  414.2 1.3 divide_convert_fusion
  415.4 80.7 %all-gather.9.cloned.1.call-done = bf16[16384,256]{1,0:T(8,128)(2,1)} async-done(((bf16[4096,256]{1,0:T(8,128)(2,1)}), bf16[16384,256]{1,0:T(8,128)(2,1)}) %all-gather.9.cloned.1.call-update) | async-done | bytes 8388624 | tf_op jit(solution)/shard_map/all_gather | solution.py:102
  496.2 6.0 %reduce_sum.92 = bf16[4096,256]{1,0:T(8,128)(2,1)S(1)} reduce(bf16[4,4096,256]{2,1,0:T(8,128)(2,1)} %bitcast.89, bf16[]{:T(256)} %constant.22.clone.1), dimensions={0}, to_apply=%region_17.18 | reduce | flops 3145728 | bytes 10485762 | tf_op jit(solution)/shard_map/reduce_sum | solution.py:102
  502.2 3.2 fusion.13
  505.7 2.0 multiply_reduce_fusion
  507.7 0.6 fusion.34
  508.3 4.6 divide_subtract_fusion
  (84 shorter events, 2.8 us)
Async XLA Ops:
  7.2 122.8 %all-gather.7.cloned.1.call-start = ((), (), s32[]{:S(2)}) async-start(), calls=%async_computation.5 | async-start | bytes 3932160 | tf_op jit(solution)/shard_map/all_gather | solution.py:47
  7.2 3.5 copy-start
  10.2 1.2 copy-start.10
  10.2 2.5 copy-start.9
  10.2 33.0 %copy-start.6 = (s32[1024,1]{0,1:T(1,128)S(1)}, s32[1024,1]{0,1:T(1,128)}, u32[]{:S(2)}) copy-start(s32[1024,1]{0,1:T(1,128)} %param.13) | copy-start | bytes 12292
  10.7 42.1 %copy-start.8 = (s32[1024]{0:T(1024)S(1)}, s32[1024]{0:T(1024)}, u32[]{:S(2)}) copy-start(s32[1024]{0:T(1024)} %param.14) | copy-start | bytes 12292
  69.1 56.1 %copy-start.2 = (bf16[1024,256]{1,0:T(8,128)(2,1)S(1)}, bf16[1024,256]{1,0:T(8,128)(2,1)}, u32[]{:S(2)}) copy-start(bf16[1024,256]{1,0:T(8,128)(2,1)} %param.10) | copy-start | bytes 1572868
  82.2 43.3 %all-to-all-start.1 = ((bf16[32,96,256]{2,1,0:T(8,128)(2,1)}), bf16[32,96,256]{2,1,0:T(8,128)(2,1)S(1)}, u32[]{:S(2)}, u32[]{:S(2)}) async-start(bf16[32,96,256]{2,1,0:T(8,128)(2,1)} %bitcast.92), calls=%async_computation.1 | async-start | bytes 3145728 | tf_op jit(solution)/shard_map/all_to_all | solution.py:37
  86.5 318.0 %reduce-scatter.2.cloned.1.call-start = ((), (), s32[]{:S(2)}) async-start(), calls=%async_computation.4 | async-start | bytes 6340608 | tf_op jit(solution)/shard_map/reduce_scatter | solution.py:100
  129.9 13.5 %copy-start.3 = (f32[1024,256]{1,0:T(8,128)S(1)}, f32[1024,256]{1,0:T(8,128)}, u32[]{:S(2)}) copy-start(f32[1024,256]{1,0:T(8,128)} %custom-call.1) | copy-start | bytes 3145732
  145.6 1.3 copy-start.11
  153.6 1.3 copy-start.11
  161.6 1.3 copy-start.11
  169.6 1.3 copy-start.11
  177.6 1.3 copy-start.11
  185.6 1.3 copy-start.11
  191.5 7.2 %copy-start.4 = (f32[1024,256]{1,0:T(8,128)}, f32[1024,256]{1,0:T(8,128)S(1)}, u32[]{:S(2)}) copy-start(f32[1024,256]{1,0:T(8,128)S(1)} %get-tuple-element.80) | copy-start | bytes 3145732
  201.8 32.3 %all-to-all-start.2 = ((bf16[32,96,256]{2,1,0:T(8,128)(2,1)}), bf16[32,96,256]{2,1,0:T(8,128)(2,1)S(1)}, u32[]{:S(2)}, u32[]{:S(2)}) async-start(bf16[32,96,256]{2,1,0:T(8,128)(2,1)} %bitcast.91), calls=%async_computation.2 | async-start | bytes 3145728 | tf_op jit(solution)/shard_map/all_to_all | solution.py:95
  211.8 284.4 %all-gather.9.cloned.1.call-start = ((), (), s32[]{:S(2)}) async-start(), calls=%async_computation.6 | async-start | bytes 10485760 | tf_op jit(solution)/shard_map/all_gather | solution.py:102
  409.8 3.9 copy-start.5
  502.2 3.5 copy-start.1
  505.7 2.0 copy-start.7
Sparse Core Ops, SparseCore 0:
  43.4 38.4 all-gather.6
  191.6 212.8 reduce-scatter.1
  413.8 82.3 all-gather.8
